TPU v7x, 32 devices: a whole 2x2x4 slice. The times are simulated.
32 devices in a mesh: aux: 4 (over z), ao: 8 (over y, x, core).
Axes of the slice: x: 2, y: 2, z: 4, core: 2. Of those that a mesh axis runs over, the one named last changes fastest.
Arguments:
- tensor: bfloat16 [64, 1024, 1024], P('aux', 'ao'), may hold values from -6 to 6
- green: bfloat16 [1024, 1024], P('aux', 'ao'), may hold values from -0.1875 to 0.1875
- tensor_mask: int32 [4, 8, 8], P('aux', 'ao'), may hold values 0 or 1
- green_mask: int32 [8, 8], P('aux', 'ao'), may hold values 0 or 1
Outputs:
- contracted: bfloat16 [64, 1024, 1024], P('aux', 'ao')
- polar: float32 [64, 16], P('aux')
All inputs are finite; a program needn't handle non-finite values. No bound on the sum of `tensor_mask` or of `green_mask` on one device may be relied on, other than what follows from the above.
Results may differ from a plain program's by a relative error of at most 0.001.
Values may be sent and summed in bfloat16 or wider, within the bound.
A program may use at most 128 MiB of HBM per device.

v0:
```python
import jax
import jax.numpy as jnp
from jax import lax
from jax.sharding import PartitionSpec as P

BLK = 128


def expand_blocks(mask, width):
    return jnp.repeat(jnp.repeat(mask, width, axis=0), width, axis=1)


def local(tensor, green, tensor_mask, green_mask):
    aux_count, row_count, orbitals = tensor.shape
    masked = tensor * expand_blocks(tensor_mask[0], BLK).astype(jnp.bfloat16)[None]
    green_local = green * expand_blocks(green_mask, BLK).astype(jnp.bfloat16)
    columns = lax.all_gather(green_local, "aux", axis=0, tiled=True)
    product = jnp.einsum(
        "pmn,nk->pmk",
        masked,
        lax.all_gather(columns, "ao", axis=1, tiled=True),
        preferred_element_type=jnp.float32,
    )
    flat_product = product.reshape(aux_count, row_count * orbitals)
    flat_masked = masked.reshape(aux_count, row_count * orbitals).astype(jnp.float32)
    partial_polar = jnp.dot(flat_product, flat_masked.T, precision=lax.Precision.HIGHEST)
    polar = lax.psum(partial_polar, "ao") / orbitals
    return (product.astype(jnp.bfloat16), polar)


def solution(mesh):
    return jax.shard_map(
        local,
        mesh=mesh,
        in_specs=(P("aux", "ao", None), P("aux", "ao"), P("aux", "ao", None), P("aux", "ao")),
        out_specs=(P("aux", "ao", None), P("aux", None)),
        check_vma=False,
    )
```

profile of v0, /device:TPU:0, one launch (start us, length us, event | category | flops | bytes accessed | tf_op | source)
XLA Modules:
  0.0 101.3 jit_solution(9471934883735907705)
XLA Ops:
  7.2 0.0 all-gather.2.cloned.1.call-start
  7.2 0.7 convert_bitcast_fusion
  7.9 0.1 broadcast_bitcast_fusion.1
  7.9 0.9 broadcast_multiply_fusion.1
  8.9 16.3 %all_gather.6 = bf16[1024,128]{1,0:T(8,128)(2,1)} all-gather(bf16[256,128]{1,0:T(8,128)(2,1)S(1)} %broadcast_multiply_fusion.1), channel_id=1, replica_groups=mesh['aux'=4,'ao'=8] {'aux'}, dimensions={0}, use_global_device_ids=true | all-gather | bytes 327680 | tf_op jit(solution)/shard_map/all_gather | solution.py:17
  25.2 0.0 all-gather.2.cloned.1.call-update
  25.2 0.7 convert_bitcast_fusion.1
  25.9 0.1 broadcast_bitcast_fusion
  26.0 4.4 %broadcast_multiply_fusion = bf16[16,128,1024]{2,1,0:T(8,128)(2,1)} fusion(bf16[16,128,1024]{2,1,0:T(8,128)(2,1)} %param.4, bf16[1024]{0:T(1024)(128)(2,1)S(1)} %broadcast_bitcast_fusion), kind=kLoop, calls=%fused_computation.5 | loop fusion | flops 2097152 | bytes 8390656 | tf_op jit(solution)/shard_map/mul | solution.py:15
  30.4 24.8 %all-gather.2.cloned.1.call-done = bf16[1024,1024]{1,0:T(8,128)(2,1)} async-done(((bf16[1024,128]{1,0:T(8,128)(2,1)}), bf16[1024,1024]{1,0:T(8,128)(2,1)}) %all-gather.2.cloned.1.call-update) | async-done | bytes 2097168 | tf_op jit(solution)/shard_map/all_gather | solution.py:21
  55.1 0.0 copy-start
  55.2 9.5 %fusion.10 = (bf16[16,128,1024]{2,1,0:T(8,128)(2,1)}, f32[16,128,1024]{2,1,0:T(8,128)S(1)}) fusion(bf16[16,128,1024]{2,1,0:T(8,128)(2,1)} %broadcast_multiply_fusion, bf16[1024,1024]{1,0:T(8,128)(2,1)} %all-gather.2.cloned.1.call-done), kind=kOutput, calls=%fused_computation.13 | convolution fusion | flops 4297064448 | bytes 18874368 | tf_op jit(solution)/shard_map/pmn,nk->pmk/dot_general | solution.py:18
  64.7 0.0 copy-done
  64.7 15.8 %fusion.5 = f32[16,16]{1,0:T(8,128)S(1)} fusion(bf16[16,128,1024]{2,1,0:T(8,128)(2,1)S(1)} %copy-done, f32[16,128,1024]{2,1,0:T(8,128)S(1)} %get-tuple-element.3), kind=kOutput, calls=%fused_computation.6 | convolution fusion | flops 402653184 | bytes 12583936 | tf_op jit(solution)/shard_map/dot_general | solution.py:26
  80.5 13.4 %psum.7 = f32[16,16]{1,0:T(8,128)S(1)} all-reduce(f32[16,16]{1,0:T(8,128)S(1)} %fusion.5), channel_id=1, replica_groups=mesh['aux'=4,'ao'=8] {'ao'}, use_global_device_ids=true, to_apply=%region_0.0 | all-reduce | flops 256 | bytes 2048 | tf_op jit(solution)/shard_map/psum | solution.py:27
  93.9 0.6 broadcast_multiply_fusion.2
Async XLA Ops:
  7.2 48.0 %all-gather.2.cloned.1.call-start = ((), (), s32[]{:S(2)}) async-start(), calls=%async_computation | async-start | bytes 2359296 | tf_op jit(solution)/shard_map/all_gather | solution.py:21
  55.1 9.5 %copy-start = (bf16[16,128,1024]{2,1,0:T(8,128)(2,1)S(1)}, bf16[16,128,1024]{2,1,0:T(8,128)(2,1)}, u32[]{:S(2)}) copy-start(bf16[16,128,1024]{2,1,0:T(8,128)(2,1)} %broadcast_multiply_fusion) | copy-start | bytes 12582916
Sparse Core Ops, SparseCore 0:
  25.3 29.7 all-gather.1
where the time goes:
time: 102 us; the launch traced here: 101 us
  blocking collectives  29.7 us (29%)
  matrix products  25.3 us (25%)
  waiting for transfers between devices  24.8 us (24%)
  between operations  14 us (14%)
  other arithmetic  7.25 us (7%)
    all_gather x1, waiting for transfers between devices, local(): lax.all_gather(columns, 'ao', axis=1, tiled=True)  24.8 us
    all_gather x1, blocking collectives, local(): columns = lax.all_gather(green_local, 'aux', axis=0, tiled=True)  16.3 us
    dot_general x1, matrix products, local(): jnp.dot(flat_product, flat_masked.T, precision=lax.Precision.HIGHEST)  15.8 us
    psum x1, blocking collectives, local(): polar = lax.psum(partial_polar, 'ao') / orbitals  13.4 us
    dot_general x1, matrix products, local(): jnp.einsum('pmn,nk->pmk', masked, lax.all_gather(columns, 'ao', axis=1, t...  9.54 us
    mul x1, other arithmetic, local(): tensor * expand_blocks(tensor_mask[0], BLK).astype(jnp.bfloat16)[None]  4.39 us
  transfers between devices with their start and end apart: 1, of which 1 were waited for; matrix products, arithmetic and copies ran while one was open for 5% of the time, Pallas kernels for 0%

commit v1 on v0

v1 whole, which is shorter than its diff:
```python
import functools

import jax
import jax.numpy as jnp
from jax import lax
from jax.experimental import pallas as pl
from jax.experimental.pallas import tpu as pltpu
from jax.sharding import PartitionSpec as P

BLK = 128
MESH = pl.DeviceIdType.MESH
TRANS_B = (((1,), (1,)), ((), ()))


def kernel(n_aux, n_ao, tensor_mask, green_mask, tensor, green, contracted, polar,
           g, rhs, tbuf, cbuf, diag, pbuf, t_sem, c_sem, send_sem, recv_sem, psend_sem, precv_sem):
    aux_count, row_count, orbitals = tbuf.shape
    depth = green.shape[0]
    n_chip = n_ao // 2
    a = lax.axis_index("aux")
    o = lax.axis_index("ao")
    chip, core = o // 2, o % 2
    sibling = chip * 2 + 1 - core

    def aux_at(k):
        return (a + k) % n_aux

    if n_chip == 4:
        cx, cy = chip % 2, chip // 2
        chips = [chip, cy * 2 + 1 - cx, (1 - cy) * 2 + cx, (1 - cy) * 2 + 1 - cx]
    else:
        chips = [(chip + t) % n_chip for t in range(n_chip)]
    cols = [c * 2 + core for c in chips]

    load = pltpu.make_async_copy(tensor, tbuf, t_sem)
    load.start()

    barrier = pltpu.get_barrier_semaphore()
    for k in range(1, n_aux):
        pl.semaphore_signal(barrier, inc=1, device_id=(aux_at(k), o), device_id_type=MESH)
    for k in range(1, n_ao):
        pl.semaphore_signal(barrier, inc=1, device_id=(a, (o + k) % n_ao), device_id_type=MESH)

    def piece(pa, po):
        return g.at[pl.ds(pl.multiple_of(pa * depth, depth), depth), pl.ds(pl.multiple_of(po * BLK, BLK), BLK)]

    for b in range(depth // BLK):
        keep = jnp.full((BLK, BLK), green_mask[b, 0].astype(jnp.float32)).astype(jnp.bfloat16)
        rows = pl.ds(pl.multiple_of(a * depth + b * BLK, BLK), BLK)
        g[rows, pl.ds(pl.multiple_of(o * BLK, BLK), BLK)] = green[b * BLK:(b + 1) * BLK, :] * keep
    pl.semaphore_wait(barrier, n_aux - 1 + n_ao - 1)

    sends = []

    def send(pa, po, to):
        copy = pltpu.make_async_remote_copy(
            src_ref=piece(pa, po), dst_ref=piece(pa, po),
            send_sem=send_sem.at[len(sends)], recv_sem=recv_sem.at[pa, po],
            device_id=to, device_id_type=MESH,
        )
        copy.start()
        sends.append(copy)

    def arrived(pa, po):
        pltpu.make_async_remote_copy(
            src_ref=piece(pa, po), dst_ref=piece(pa, po),
            send_sem=send_sem.at[0], recv_sem=recv_sem.at[pa, po],
            device_id=(a, sibling), device_id_type=MESH,
        ).wait_recv()

    def to_chips(k):
        direct = 3 if n_chip == 4 else n_chip
        for t in range(1, direct):
            send(aux_at(k), o, (a, cols[t]))
        send(aux_at(k), o, (a, sibling))

    def forward(k):
        if n_chip == 4:
            first, second = (1, 2) if k % 2 == 0 else (2, 1)
            arrived(aux_at(k), cols[first])
            send(aux_at(k), cols[first], (a, cols[second]))
            send(aux_at(k), cols[first], (a, sibling))
            arrived(aux_at(k), cols[second])
            send(aux_at(k), cols[second], (a, sibling))

    def finish(t, k):
        arrived(aux_at(k), cols[t])
        send(aux_at(k), cols[t], (a, sibling))

    def multiply(t):
        for k in range(n_aux):
            arrived(aux_at(k), chips[t] * 2 + 1 - core)
        lanes = pl.ds(pl.multiple_of(chips[t] * 2 * BLK, 2 * BLK), 2 * BLK)
        for b in range(n_ao):
            keep = jnp.full((BLK, 2 * BLK), tensor_mask[0, 0, b].astype(jnp.float32)).astype(jnp.bfloat16)
            rhs[b * BLK:(b + 1) * BLK, :] = g[b * BLK:(b + 1) * BLK, lanes] * keep
        keep_lanes = jnp.concatenate(
            [jnp.full((16 * aux_count, BLK), tensor_mask[0, 0, chips[t] * 2 + i].astype(jnp.float32)) for i in range(2)],
            axis=1,
        ).astype(jnp.bfloat16)

        def tile(j, carry):
            rows = pl.ds(pl.multiple_of(j * 32, 32), 32)
            left = tbuf[:, rows, :].reshape(aux_count * 32, orbitals)
            product = jnp.dot(left, rhs[...], preferred_element_type=jnp.float32)
            high = product.astype(jnp.bfloat16)
            low = (product - high.astype(jnp.float32)).astype(jnp.bfloat16)
            high = high.reshape(aux_count, 32, 2 * BLK)
            low = low.reshape(aux_count, 32, 2 * BLK)
            cbuf[:, rows, lanes] = high
            right = tbuf[:, rows, lanes]
            total = diag[...]
            for s in range(2):
                part = slice(s * 16, s * 16 + 16)
                kept = right[:, part].reshape(aux_count * 16, 2 * BLK) * keep_lanes
                for half in (high, low):
                    total += lax.dot_general(
                        half[:, part].reshape(aux_count * 16, 2 * BLK), kept, TRANS_B,
                        preferred_element_type=jnp.float32,
                    )
            diag[...] = total
            return carry

        lax.fori_loop(0, row_count // 32, tile, 0)
        store = pltpu.make_async_copy(cbuf.at[:, :, lanes], contracted.at[:, :, lanes], c_sem.at[t])
        store.start()
        return store

    for k in range(1, n_aux):
        send(a, o, (aux_at(k), o))
    to_chips(0)
    diag[...] = jnp.zeros_like(diag)
    for k in range(1, n_aux):
        arrived(aux_at(k), o)
        to_chips(k)
        forward(k - 1)
    load.wait()
    stores = [multiply(0)]
    forward(n_aux - 1)
    for t in range(1, n_chip):
        ahead = [t + 1] if n_chip == 4 else [t]
        for late in ahead:
            if n_chip != 4 or late == 3:
                for k in range(n_aux):
                    finish(late, k)
        stores.append(multiply(t))

    size = 16 * aux_count
    row = lax.broadcasted_iota(jnp.int32, (size, size), 0)
    col = lax.broadcasted_iota(jnp.int32, (size, size), 1)
    same = jnp.where(row % 16 == col % 16, diag[...], 0.0)
    by_row = jnp.sum(same.reshape(aux_count, 16, size), axis=1)
    spread = lax.broadcasted_iota(jnp.int32, (size, BLK), 0) // 16 == lax.broadcasted_iota(jnp.int32, (size, BLK), 1)
    pbuf[o] = jnp.dot(by_row, spread.astype(jnp.float32), precision=lax.Precision.HIGHEST,
                      preferred_element_type=jnp.float32)
    swaps = []
    for k in range(1, n_ao):
        swap = pltpu.make_async_remote_copy(
            src_ref=pbuf.at[o], dst_ref=pbuf.at[o],
            send_sem=psend_sem.at[k], recv_sem=precv_sem.at[o],
            device_id=(a, (o + k) % n_ao), device_id_type=MESH,
        )
        swap.start()
        swaps.append(swap)
    for copy in sends:
        copy.wait_send()
    for store in stores:
        store.wait()
    for k in range(1, n_ao):
        other = (o + k) % n_ao
        pltpu.make_async_remote_copy(
            src_ref=pbuf.at[other], dst_ref=pbuf.at[other],
            send_sem=psend_sem.at[k], recv_sem=precv_sem.at[other],
            device_id=(a, other), device_id_type=MESH,
        ).wait_recv()
    for swap in swaps:
        swap.wait_send()
    whole = pbuf[0]
    for i in range(1, n_ao):
        whole += pbuf[i]
    polar[...] = whole[:, :aux_count] * (1.0 / orbitals)


def local(n_aux, n_ao, tensor, green, tensor_mask, green_mask):
    aux_count, row_count, orbitals = tensor.shape
    bf16, f32 = jnp.bfloat16, jnp.float32
    n_chip = n_ao // 2
    n_sends = n_aux - 1 + n_aux * ((n_chip - 1) + n_chip)
    dma = pltpu.SemaphoreType.DMA
    return pl.pallas_call(
        functools.partial(kernel, n_aux, n_ao),
        out_shape=(
            jax.ShapeDtypeStruct(tensor.shape, bf16),
            jax.ShapeDtypeStruct((aux_count, aux_count), f32),
        ),
        in_specs=[
            pl.BlockSpec(memory_space=pltpu.SMEM),
            pl.BlockSpec(memory_space=pltpu.SMEM),
            pl.BlockSpec(memory_space=pl.ANY),
            pl.BlockSpec(memory_space=pltpu.VMEM),
        ],
        out_specs=(pl.BlockSpec(memory_space=pl.ANY), pl.BlockSpec(memory_space=pltpu.VMEM)),
        scratch_shapes=[
            pltpu.VMEM((orbitals, orbitals), bf16),
            pltpu.VMEM((orbitals, 2 * BLK), bf16),
            pltpu.VMEM(tensor.shape, bf16),
            pltpu.VMEM(tensor.shape, bf16),
            pltpu.VMEM((16 * aux_count, 16 * aux_count), f32),
            pltpu.VMEM((n_ao, aux_count, BLK), f32),
            dma(()),
            dma((n_chip,)),
            dma((n_sends,)),
            dma((n_aux, n_ao)),
            dma((n_ao,)),
            dma((n_ao,)),
        ],
        compiler_params=pltpu.CompilerParams(
            collective_id=0, has_side_effects=True, vmem_limit_bytes=48 * 2**20
        ),
    )(tensor_mask, green_mask, tensor, green)


def solution(mesh):
    return jax.shard_map(
        functools.partial(local, mesh.shape["aux"], mesh.shape["ao"]),
        mesh=mesh,
        in_specs=(P("aux", "ao", None), P("aux", "ao"), P("aux", "ao", None), P("aux", "ao")),
        out_specs=(P("aux", "ao", None), P("aux", None)),
        check_vma=False,
    )
```

time: 102 us -> 43.3 us (0.42)
  Pallas kernels: 0 us -> 37.3 us
  blocking collectives: 29.7 us -> 0 us
  matrix products: 25.3 us -> 0 us
  waiting for transfers between devices: 24.8 us -> 0 us
  between operations: 14 us -> 0.64 us
  other arithmetic: 7.25 us -> 0 us
  local copies, waits for them, and re-layouts: 0.15 us -> 4.85 us
    pallas_call x0 -> x1, Pallas kernels: none -> 37.3 us  [local(): pl.pallas_call(functools.partial(kernel, n_aux, n_ao), out_shape=(jax.Sha...]
    dot_general x2 -> x0, matrix products: 25.3 us -> none  [the longest x1 15.8 us: local(): jnp.dot(flat_product, flat_masked.T, precision=lax.Precision.HIGHEST)]
    all_gather x1 -> x0, waiting for transfers between devices: 24.8 us -> none  [local(): lax.all_gather(columns, 'ao', axis=1, tiled=True)]
    all_gather x1 -> x0, blocking collectives: 16.3 us -> none  [local(): columns = lax.all_gather(green_local, 'aux', axis=0, tiled=True)]
    psum x1 -> x0, blocking collectives: 13.4 us -> none  [local(): polar = lax.psum(partial_polar, 'ao') / orbitals]
    mul x2 -> x0, other arithmetic: 5.33 us -> none  [the longest x1 4.39 us: local(): tensor * expand_blocks(tensor_mask[0], BLK).astype(jnp.bfloat16)[None]]
    unnamed x2 -> x7, local copies, waits for them, and re-layouts: 0.01 us -> 4.85 us
    convert_element_type x2 -> x0, other arithmetic: 1.32 us -> none  [the longest x1 0.66 us: local(): expand_blocks(tensor_mask[0], BLK).astype(jnp.bfloat16)[None]]
  transfers between devices with their start and end apart: 1 -> 0, of which waited for: 1 -> 0; matrix products, arithmetic and copies ran while one was open for 5% -> 0% of each run, Pallas kernels for 0% -> 0%
where the time goes in v1:
time: 43.3 us; the launch traced here: 42.8 us
  Pallas kernels  37.3 us (86%)
  local copies, waits for them, and re-layouts  4.85 us (11%)
  between operations  0.64 us (1%)
    pallas_call x1, Pallas kernels, local(): pl.pallas_call(functools.partial(kernel, n_aux, n_ao), out_shape=(jax.Sha...  37.3 us
    unnamed x7, local copies, waits for them, and re-layouts  4.85 us

profile of v1, /device:TPU:0, one launch (start us, length us, event | category | flops | bytes accessed | tf_op | source)
XLA Modules:
  0.0 42.8 jit_solution(12745194291997986511)
XLA Ops:
  0.6 0.7 %copy.6.green_mask = s32[2,1]{1,0:T(2,128)S(1)} copy(s32[2,1]{0,1:T(1,128)} %param.7) | data formatting | bytes 16 | tf_op args[3]
  1.4 0.0 copy-start
  1.4 0.8 %copy-done = bf16[256,128]{1,0:T(8,128)(2,1)S(1)} copy-done((bf16[256,128]{1,0:T(8,128)(2,1)S(1)}, bf16[256,128]{1,0:T(8,128)(2,1)}, u32[]{:S(2)}) %copy-start) | copy-done | bytes 65560
  2.2 0.0 copy-start.1
  2.2 0.7 %copy-done.1 = s32[1,1,8]{2,1,0:T(1,128)S(1)} copy-done((s32[1,1,8]{2,1,0:T(1,128)S(1)}, s32[1,1,8]{2,1,0:T(1,128)}, u32[]{:S(2)}) %copy-start.1) | copy-done | bytes 56
  2.9 37.3 %shard_map.59 = (bf16[16,128,1024]{2,1,0:T(8,128)(2,1)S(1)}, f32[16,16]{1,0:T(8,128)S(1)}) custom-call(s32[1,1,8]{2,1,0:T(1,128)S(1)} %copy-done.1, s32[2,1]{1,0:T(2,128)S(1)} %copy.6.green_mask, bf16[16,128,1024]{2,1,0:T(8,128)(2,1)} %tensor.1, bf16[256,128]{1,0:T(8,128)(2,1)S(1)} %copy-done), custom_call_target="tpu_custom_call" | custom-call | tf_op jit(solution)/shard_map/pallas_call | solution.py:190
  40.2 2.0 %copy.9 = bf16[16,128,1024]{2,1,0:T(8,128)(2,1)} copy(bf16[16,128,1024]{2,1,0:T(8,128)(2,1)S(1)} %get-tuple-element.4) | data formatting | bytes 8388608
  42.2 0.6 %copy.10 = f32[16,16]{1,0:T(8,128)} copy(f32[16,16]{1,0:T(8,128)S(1)} %get-tuple-element.5) | data formatting | bytes 2048
Async XLA Ops:
  1.4 0.8 %copy-start = (bf16[256,128]{1,0:T(8,128)(2,1)S(1)}, bf16[256,128]{1,0:T(8,128)(2,1)}, u32[]{:S(2)}) copy-start(bf16[256,128]{1,0:T(8,128)(2,1)} %green.1) | copy-start | bytes 196612
  2.2 0.7 %copy-start.1 = (s32[1,1,8]{2,1,0:T(1,128)S(1)}, s32[1,1,8]{2,1,0:T(1,128)}, u32[]{:S(2)}) copy-start(s32[1,1,8]{2,1,0:T(1,128)} %tensor_mask.1) | copy-start | bytes 100

commit v2 on v1

v2 whole, which is shorter than its diff:
```python
import functools

import jax
import jax.numpy as jnp
from jax import lax
from jax.experimental import pallas as pl
from jax.experimental.pallas import tpu as pltpu
from jax.sharding import PartitionSpec as P

BLK = 128
TILE = 64
MESH = pl.DeviceIdType.MESH
TRANS_B = (((1,), (1,)), ((), ()))


def kernel(n_aux, n_ao, tensor_mask, green_mask, tensor, green, contracted, polar,
           g, rhs, tbuf, diag, pbuf, own, g_mask, t_mask, lane_mask, t_sem, in_sem, send_sem, recv_sem, psend_sem, precv_sem):
    aux_count, row_count, orbitals = tbuf.shape
    depth = green.shape[0]
    n_chip = n_ao // 2
    a = lax.axis_index("aux")
    o = lax.axis_index("ao")
    chip, core = o // 2, o % 2
    sibling = chip * 2 + 1 - core

    short = jnp.minimum(a, n_aux - 1 - a)
    from_left = [None] + [jnp.where(k <= 2 * short, k % 2, (2 * a >= n_aux).astype(jnp.int32)) for k in range(1, n_aux)]
    pieces = [a] + [
        a + jnp.where(k <= 2 * short, (k + 1) // 2, k - short) * (1 - 2 * from_left[k]) for k in range(1, n_aux)
    ]

    def aux_at(k):
        return pieces[k]

    if n_chip == 4:
        cx, cy = chip % 2, chip // 2
        chips = [chip, cy * 2 + 1 - cx, (1 - cy) * 2 + cx, (1 - cy) * 2 + 1 - cx]
    else:
        chips = [(chip + t) % n_chip for t in range(n_chip)]
    cols = [c * 2 + core for c in chips]

    load = pltpu.make_async_copy(tensor, tbuf, t_sem)
    loads = [
        pltpu.make_async_copy(green, own, in_sem.at[0]),
        pltpu.make_async_copy(green_mask, g_mask, in_sem.at[1]),
        pltpu.make_async_copy(tensor_mask, t_mask, in_sem.at[2]),
    ]
    for copy in loads:
        copy.start()
    load.start()

    barrier = pltpu.get_barrier_semaphore()
    for k in range(1, n_aux):
        pl.semaphore_signal(barrier, inc=1, device_id=(aux_at(k), o), device_id_type=MESH)
    for k in range(1, n_ao):
        pl.semaphore_signal(barrier, inc=1, device_id=(a, (o + k) % n_ao), device_id_type=MESH)

    def piece(pa, po):
        return g.at[po, pl.ds(pl.multiple_of(pa * depth, depth), depth), :]

    for copy in loads:
        copy.wait()
    for b in range(depth // BLK):
        keep = jnp.broadcast_to(g_mask[b:b + 1, 0:1].astype(jnp.float32), (BLK, BLK)).astype(jnp.bfloat16)
        rows = pl.ds(pl.multiple_of(a * depth + b * BLK, BLK), BLK)
        g[o, rows, :] = own[b * BLK:(b + 1) * BLK, :] * keep
    for b in range(n_ao):
        lane_mask[:, b * BLK:(b + 1) * BLK] = jnp.broadcast_to(
            t_mask[0, 0:1, b:b + 1].astype(jnp.float32), lane_mask[:, b * BLK:(b + 1) * BLK].shape
        )
    pl.semaphore_wait(barrier, n_ao - 1 + n_aux - 1)

    sends = []

    def send(pa, po, to):
        copy = pltpu.make_async_remote_copy(
            src_ref=piece(pa, po), dst_ref=piece(pa, po),
            send_sem=send_sem.at[len(sends)], recv_sem=recv_sem.at[pa, po],
            device_id=to, device_id_type=MESH,
        )
        copy.start()
        sends.append(copy)

    def arrived(pa, po):
        pltpu.make_async_remote_copy(
            src_ref=piece(pa, po), dst_ref=piece(pa, po),
            send_sem=send_sem.at[0], recv_sem=recv_sem.at[pa, po],
            device_id=(a, sibling), device_id_type=MESH,
        ).wait_recv()

    cross = n_chip == 4

    def to_chips(k):
        for t in range(1, 3 if cross and k > 0 else n_chip):
            send(aux_at(k), o, (a, cols[t]))
        send(aux_at(k), o, (a, sibling))

    def finish(t, k):
        arrived(aux_at(k), cols[t])
        send(aux_at(k), cols[t], (a, sibling))

    def multiply(t):
        for k in range(n_aux):
            arrived(aux_at(k), chips[t] * 2 + 1 - core)
        lanes = pl.ds(pl.multiple_of(chips[t] * 2 * BLK, 2 * BLK), 2 * BLK)
        for b in range(n_ao):
            keep = jnp.broadcast_to(lane_mask[0:1, b * BLK:b * BLK + 1], (BLK, BLK)).astype(jnp.bfloat16)
            for i in range(2):
                rhs[b * BLK:(b + 1) * BLK, i * BLK:(i + 1) * BLK] = g[chips[t] * 2 + i, b * BLK:(b + 1) * BLK, :] * keep
        keep_lanes = jnp.broadcast_to(lane_mask[0:1, lanes], (16 * aux_count, 2 * BLK)).astype(jnp.bfloat16)

        def tile(j, carry):
            rows = pl.ds(pl.multiple_of(j * TILE, TILE), TILE)
            left_rows = tbuf[:, rows, :].reshape(aux_count * TILE, orbitals)
            product = jnp.dot(left_rows, rhs[...], preferred_element_type=jnp.float32)
            high = product.astype(jnp.bfloat16)
            low = (product - high.astype(jnp.float32)).astype(jnp.bfloat16)
            high = high.reshape(aux_count, TILE, 2 * BLK)
            low = low.reshape(aux_count, TILE, 2 * BLK)
            contracted[:, rows, lanes] = high
            right_rows = tbuf[:, rows, lanes]
            total = diag[...]
            for s in range(TILE // 16):
                part = slice(s * 16, s * 16 + 16)
                kept = right_rows[:, part].reshape(aux_count * 16, 2 * BLK) * keep_lanes
                halves = jnp.concatenate([high[:, part], low[:, part]], axis=0).reshape(aux_count * 32, 2 * BLK)
                total += lax.dot_general(halves, kept, TRANS_B, preferred_element_type=jnp.float32)
            diag[...] = total
            return carry

        lax.fori_loop(0, row_count // TILE, tile, 0)

    for k in range(1, n_aux):
        send(a, o, (aux_at(k), o))
    to_chips(0)
    diag[...] = jnp.zeros_like(diag)
    if cross:
        finish(3, 0)
        for k in range(1, n_aux):
            send(a, cols[3], (aux_at(k), o))
    for k in range(1, n_aux):
        arrived(aux_at(k), o)
        to_chips(k)
    load.wait()
    multiply(0)
    for t in range(1, n_chip):
        if cross and t == 1:
            for late in (1, 2):
                for k in range(n_aux):
                    finish(late, k)
        if cross and t == 2:
            for k in range(1, n_aux):
                finish(3, k)
        if not cross:
            for k in range(n_aux):
                finish(t, k)
        multiply(t)

    size = 16 * aux_count
    row = lax.broadcasted_iota(jnp.int32, (size, size), 0)
    col = lax.broadcasted_iota(jnp.int32, (size, size), 1)
    same = jnp.where(row % 16 == col % 16, diag[0:size, :] + diag[size:, :], 0.0)
    by_row = jnp.sum(same.reshape(aux_count, 16, size), axis=1)
    spread = lax.broadcasted_iota(jnp.int32, (size, BLK), 0) // 16 == lax.broadcasted_iota(jnp.int32, (size, BLK), 1)
    pbuf[o] = jnp.dot(by_row, spread.astype(jnp.float32), precision=lax.Precision.HIGHEST,
                      preferred_element_type=jnp.float32)
    swaps = []
    for k in range(1, n_ao):
        swap = pltpu.make_async_remote_copy(
            src_ref=pbuf.at[o], dst_ref=pbuf.at[o],
            send_sem=psend_sem.at[k], recv_sem=precv_sem.at[o],
            device_id=(a, (o + k) % n_ao), device_id_type=MESH,
        )
        swap.start()
        swaps.append(swap)
    for copy in sends:
        copy.wait_send()
    for k in range(1, n_ao):
        other = (o + k) % n_ao
        pltpu.make_async_remote_copy(
            src_ref=pbuf.at[other], dst_ref=pbuf.at[other],
            send_sem=psend_sem.at[k], recv_sem=precv_sem.at[other],
            device_id=(a, other), device_id_type=MESH,
        ).wait_recv()
    for swap in swaps:
        swap.wait_send()
    whole = pbuf[0]
    for i in range(1, n_ao):
        whole += pbuf[i]
    polar[...] = whole[:, :aux_count] * (1.0 / orbitals)


def local(n_aux, n_ao, tensor, green, tensor_mask, green_mask):
    aux_count, row_count, orbitals = tensor.shape
    bf16, f32 = jnp.bfloat16, jnp.float32
    n_chip = n_ao // 2
    n_sends = n_aux - 1 + n_aux * ((n_chip - 1) + n_chip)
    dma = pltpu.SemaphoreType.DMA
    return pl.pallas_call(
        functools.partial(kernel, n_aux, n_ao),
        out_shape=(
            jax.ShapeDtypeStruct(tensor.shape, bf16),
            jax.ShapeDtypeStruct((aux_count, aux_count), f32),
        ),
        in_specs=[
            pl.BlockSpec(memory_space=pltpu.HBM),
            pl.BlockSpec(memory_space=pltpu.HBM),
            pl.BlockSpec(memory_space=pltpu.HBM),
            pl.BlockSpec(memory_space=pltpu.HBM),
        ],
        out_specs=(pl.BlockSpec(memory_space=pltpu.VMEM), pl.BlockSpec(memory_space=pltpu.VMEM)),
        scratch_shapes=[
            pltpu.VMEM((n_ao, orbitals, BLK), bf16),
            pltpu.VMEM((orbitals, 2 * BLK), bf16),
            pltpu.VMEM(tensor.shape, bf16),
            pltpu.VMEM((32 * aux_count, 16 * aux_count), f32),
            pltpu.VMEM((n_ao, aux_count, BLK), f32),
            pltpu.VMEM(green.shape, bf16),
            pltpu.VMEM(green_mask.shape, jnp.int32),
            pltpu.VMEM(tensor_mask.shape, jnp.int32),
            pltpu.VMEM((8, orbitals), f32),
            dma(()),
            dma((3,)),
            dma((n_sends,)),
            dma((n_aux, n_ao)),
            dma((n_ao,)),
            dma((n_ao,)),
        ],
        compiler_params=pltpu.CompilerParams(
            collective_id=0, has_side_effects=True, vmem_limit_bytes=48 * 2**20
        ),
    )(tensor_mask, green_mask, tensor, green)


def solution(mesh):
    return jax.shard_map(
        functools.partial(local, mesh.shape["aux"], mesh.shape["ao"]),
        mesh=mesh,
        in_specs=(P("aux", "ao", None), P("aux", "ao"), P("aux", "ao", None), P("aux", "ao")),
        out_specs=(P("aux", "ao", None), P("aux", None)),
        check_vma=False,
    )
```

time: 43.3 us -> 38.1 us (0.88)
  Pallas kernels: 37.3 us -> 32.4 us
    pallas_call x1, Pallas kernels: 37.3 us -> 32.4 us  [local(): pl.pallas_call(functools.partial(kernel, n_aux, n_ao), out_shape=(jax.Sha...]
where the time goes in v2:
time: 38.1 us; the launch traced here: 37.9 us
  Pallas kernels  32.4 us (85%)
  local copies, waits for them, and re-layouts  4.85 us (13%)
  between operations  0.64 us (2%)
    pallas_call x1, Pallas kernels, local(): pl.pallas_call(functools.partial(kernel, n_aux, n_ao), out_shape=(jax.Sha...  32.4 us
    unnamed x7, local copies, waits for them, and re-layouts  4.85 us

profile of v2, /device:TPU:0, one launch (start us, length us, event | category | flops | bytes accessed | tf_op | source)
XLA Modules:
  0.0 37.9 jit_solution(5206017398474700162)
XLA Ops:
  0.6 0.7 %copy.6.green_mask = s32[2,1]{1,0:T(2,128)S(1)} copy(s32[2,1]{0,1:T(1,128)} %param.7) | data formatting | bytes 16 | tf_op args[3]
  1.4 0.0 copy-start
  1.4 0.8 %copy-done = bf16[256,128]{1,0:T(8,128)(2,1)S(1)} copy-done((bf16[256,128]{1,0:T(8,128)(2,1)S(1)}, bf16[256,128]{1,0:T(8,128)(2,1)}, u32[]{:S(2)}) %copy-start) | copy-done | bytes 65560
  2.2 0.0 copy-start.1
  2.2 0.7 %copy-done.1 = s32[1,1,8]{2,1,0:T(1,128)S(1)} copy-done((s32[1,1,8]{2,1,0:T(1,128)S(1)}, s32[1,1,8]{2,1,0:T(1,128)}, u32[]{:S(2)}) %copy-start.1) | copy-done | bytes 56
  2.9 32.4 %shard_map.59 = (bf16[16,128,1024]{2,1,0:T(8,128)(2,1)S(1)}, f32[16,16]{1,0:T(8,128)S(1)}) custom-call(s32[1,1,8]{2,1,0:T(1,128)S(1)} %copy-done.1, s32[2,1]{1,0:T(2,128)S(1)} %copy.6.green_mask, bf16[16,128,1024]{2,1,0:T(8,128)(2,1)} %tensor.1, bf16[256,128]{1,0:T(8,128)(2,1)S(1)} %copy-done), custom_call_target="tpu_custom_call" | custom-call | tf_op jit(solution)/shard_map/pallas_call | solution.py:199
  35.3 2.0 %copy.9 = bf16[16,128,1024]{2,1,0:T(8,128)(2,1)} copy(bf16[16,128,1024]{2,1,0:T(8,128)(2,1)S(1)} %get-tuple-element.4) | data formatting | bytes 8388608
  37.3 0.6 %copy.10 = f32[16,16]{1,0:T(8,128)} copy(f32[16,16]{1,0:T(8,128)S(1)} %get-tuple-element.5) | data formatting | bytes 2048
Async XLA Ops:
  1.4 0.8 %copy-start = (bf16[256,128]{1,0:T(8,128)(2,1)S(1)}, bf16[256,128]{1,0:T(8,128)(2,1)}, u32[]{:S(2)}) copy-start(bf16[256,128]{1,0:T(8,128)(2,1)} %green.1) | copy-start | bytes 196612
  2.2 0.7 %copy-start.1 = (s32[1,1,8]{2,1,0:T(1,128)S(1)}, s32[1,1,8]{2,1,0:T(1,128)}, u32[]{:S(2)}) copy-start(s32[1,1,8]{2,1,0:T(1,128)} %tensor_mask.1) | copy-start | bytes 100

commit v3 on v2

--- a/solution.py
+++ b/solution.py
@@ -8,7 +8,7 @@
 from jax.sharding import PartitionSpec as P
 
 BLK = 128
-TILE = 64
+TILE = 32
 MESH = pl.DeviceIdType.MESH
 TRANS_B = (((1,), (1,)), ((), ()))
 
@@ -119,16 +119,18 @@
             low = low.reshape(aux_count, TILE, 2 * BLK)
             contracted[:, rows, lanes] = high
             right_rows = tbuf[:, rows, lanes]
-            total = diag[...]
-            for s in range(TILE // 16):
-                part = slice(s * 16, s * 16 + 16)
-                kept = right_rows[:, part].reshape(aux_count * 16, 2 * BLK) * keep_lanes
-                halves = jnp.concatenate([high[:, part], low[:, part]], axis=0).reshape(aux_count * 32, 2 * BLK)
-                total += lax.dot_general(halves, kept, TRANS_B, preferred_element_type=jnp.float32)
-            diag[...] = total
+            parts = [slice(s * 16, s * 16 + 16) for s in range(TILE // 16)]
+            kept = jnp.concatenate(
+                [right_rows[:, part].reshape(aux_count * 16, 2 * BLK) * keep_lanes for part in parts], axis=1
+            )
+            halves = jnp.concatenate(
+                [jnp.concatenate([high[:, part], low[:, part]], axis=0).reshape(aux_count * 32, 2 * BLK)
+                 for part in parts], axis=1,
+            )
+            diag[...] += lax.dot_general(halves, kept, TRANS_B, preferred_element_type=jnp.float32)
             return carry
 
-        lax.fori_loop(0, row_count // TILE, tile, 0)
+        lax.fori_loop(0, row_count // TILE, tile, 0, unroll=True)
 
     for k in range(1, n_aux):
         send(a, o, (aux_at(k), o))

time: 38.1 us -> 34.9 us (0.916)
  Pallas kernels: 32.4 us -> 29.2 us
    pallas_call x1, Pallas kernels: 32.4 us -> 29.2 us  [local(): pl.pallas_call(functools.partial(kernel, n_aux, n_ao), out_shape=(jax.Sha...]
where the time goes in v3:
time: 34.9 us; the launch traced here: 34.7 us
  Pallas kernels  29.2 us (84%)
  local copies, waits for them, and re-layouts  4.85 us (14%)
  between operations  0.64 us (2%)
    pallas_call x1, Pallas kernels, local(): pl.pallas_call(functools.partial(kernel, n_aux, n_ao), out_shape=(jax.Sha...  29.2 us
    unnamed x7, local copies, waits for them, and re-layouts  4.85 us

profile of v3, /device:TPU:0, one launch (start us, length us, event | category | flops | bytes accessed | tf_op | source)
XLA Modules:
  0.0 34.7 jit_solution(3875962174210521282)
XLA Ops:
  0.6 0.7 %copy.6.green_mask = s32[2,1]{1,0:T(2,128)S(1)} copy(s32[2,1]{0,1:T(1,128)} %param.7) | data formatting | bytes 16 | tf_op args[3]
  1.4 0.0 copy-start
  1.4 0.8 %copy-done = bf16[256,128]{1,0:T(8,128)(2,1)S(1)} copy-done((bf16[256,128]{1,0:T(8,128)(2,1)S(1)}, bf16[256,128]{1,0:T(8,128)(2,1)}, u32[]{:S(2)}) %copy-start) | copy-done | bytes 65560
  2.2 0.0 copy-start.1
  2.2 0.7 %copy-done.1 = s32[1,1,8]{2,1,0:T(1,128)S(1)} copy-done((s32[1,1,8]{2,1,0:T(1,128)S(1)}, s32[1,1,8]{2,1,0:T(1,128)}, u32[]{:S(2)}) %copy-start.1) | copy-done | bytes 56
  2.9 29.2 %shard_map.59 = (bf16[16,128,1024]{2,1,0:T(8,128)(2,1)S(1)}, f32[16,16]{1,0:T(8,128)S(1)}) custom-call(s32[1,1,8]{2,1,0:T(1,128)S(1)} %copy-done.1, s32[2,1]{1,0:T(2,128)S(1)} %copy.6.green_mask, bf16[16,128,1024]{2,1,0:T(8,128)(2,1)} %tensor.1, bf16[256,128]{1,0:T(8,128)(2,1)S(1)} %copy-done), custom_call_target="tpu_custom_call" | custom-call | tf_op jit(solution)/shard_map/pallas_call | solution.py:201
  32.1 2.0 %copy.9 = bf16[16,128,1024]{2,1,0:T(8,128)(2,1)} copy(bf16[16,128,1024]{2,1,0:T(8,128)(2,1)S(1)} %get-tuple-element.4) | data formatting | bytes 8388608
  34.1 0.6 %copy.10 = f32[16,16]{1,0:T(8,128)} copy(f32[16,16]{1,0:T(8,128)S(1)} %get-tuple-element.5) | data formatting | bytes 2048
Async XLA Ops:
  1.4 0.8 %copy-start = (bf16[256,128]{1,0:T(8,128)(2,1)S(1)}, bf16[256,128]{1,0:T(8,128)(2,1)}, u32[]{:S(2)}) copy-start(bf16[256,128]{1,0:T(8,128)(2,1)} %green.1) | copy-start | bytes 196612
  2.2 0.7 %copy-start.1 = (s32[1,1,8]{2,1,0:T(1,128)S(1)}, s32[1,1,8]{2,1,0:T(1,128)}, u32[]{:S(2)}) copy-start(s32[1,1,8]{2,1,0:T(1,128)} %tensor_mask.1) | copy-start | bytes 100
